TPU v7x, 32 devices: a whole 2x2x4 slice. The times are simulated.
32 devices in a mesh: grp: 2 (over y), cuts: 4 (over z), space: 4 (over x, core).
Axes of the slice: x: 2, y: 2, z: 4, core: 2. Of those that a mesh axis runs over, the one named last changes fastest.
Arguments:
- left_modes: float32 [8, 1024, 1024], P(('grp', 'cuts'), None, 'space'), parts along dimension 0, may hold values from -0.25 to 0.25
- right_modes: float32 [8, 1024, 1024], P(('grp', 'cuts'), None, 'space'), parts along dimension 0, may hold values from -6 to 6
- momenta: int32 [4, 3], replicated, may hold values from -2 to 2
- partners: int32 [4], replicated, may hold values from 0 to 3, as said below
Outputs:
- meson_field: float32 [8, 1024, 4, 1024], P(('grp', 'cuts'), 'space'), parts along dimension 0
- product: float32 [8, 1024, 4, 1024], P(('grp', 'cuts'), 'space'), parts along dimension 0
There are 2 independent parts, one for each index of `grp`. A program takes and returns all parts, laid end to end along the dimension named above; an argument that names none is the same for every part. Nothing has to cross between parts.
Inputs may be any that keep to these rules, and one draw needn't show every extreme that they name: `partners`: every slice is named exactly once.
All inputs are finite; a program needn't handle non-finite values.
Results may differ from a plain program's by a relative error of at most 0.00011.
Values sent between devices are 32-bit elements; how exact they have to be, the bound alone decides.
A program may use at most 64 MiB of HBM per device.

v0:
```python
import math

import jax
import jax.numpy as jnp
from jax import lax
from jax.sharding import PartitionSpec as P

MODES = 1024


def partner(value, axis, bit):
    mask = 2**bit
    pairs = [(source, source ^ mask) for source in range(lax.axis_size(axis))]
    return lax.ppermute(value, axis, pairs)


def phase_table(momenta, offset, amount, site_total):
    global_site = offset + jnp.arange(amount, dtype=jnp.int32)
    coord_x = global_site % 8
    coord_y = global_site // 8 % 8
    coord_z = global_site // 64
    depth = site_total // 64
    numerator = (
        (momenta[:, 0:1] * coord_x[None] + momenta[:, 1:2] * coord_y[None]) * depth
        + momenta[:, 2:3] * coord_z[None] * 8
    ) % (8 * depth)
    return jnp.cos(2.0 * math.pi * numerator.astype(jnp.float32) / (8 * depth))


def on_device(left_modes, right_modes, momenta, partners):
    left_local = left_modes[0]
    right_local = right_modes[0]
    mode_total = left_local.shape[0]
    site_local = left_local.shape[1]
    space_size = lax.axis_size("space")
    site_total = site_local * space_size
    row_count = mode_total // space_size
    space_index = lax.axis_index("space")
    slice_index = lax.axis_index("cuts")
    half_groups = space_size // 2
    low_bit = space_index % 2
    grouped = left_local.reshape(half_groups, 2, row_count, site_local)
    left_mine = lax.dynamic_index_in_dim(grouped, low_bit, 1, keepdims=False)
    left_other = lax.dynamic_index_in_dim(grouped, 1 - low_bit, 1, keepdims=False)
    left_recv, right_recv = partner((left_other, right_local), "space", 0)
    neighbour = space_index + 1 - 2 * low_bit
    phase_mine = phase_table(momenta, space_index * site_local, site_local, site_total)
    phase_other = phase_table(momenta, neighbour * site_local, site_local, site_total)
    left_pair = jnp.concatenate([left_mine, left_recv], axis=2).reshape(
        half_groups * row_count, 2 * site_local
    )
    right_pair = jnp.concatenate([right_local, right_recv], axis=1)
    phase_pair = jnp.concatenate([phase_mine, phase_other], axis=1)
    weighted = left_pair[:, None, :] * phase_pair[None]
    partial_sum = jnp.einsum("max,nx->man", weighted, right_pair, precision=lax.Precision.HIGHEST)
    partial_sum = partial_sum.reshape(half_groups, row_count, momenta.shape[0], mode_total)
    bit_count = space_size.bit_length() - 1
    for bit_number in range(bit_count - 1, 0, -1):
        which_bit = space_index // 2**bit_number % 2
        split_sum = partial_sum.reshape((2, partial_sum.shape[0] // 2) + partial_sum.shape[1:])
        keeping = lax.dynamic_index_in_dim(split_sum, which_bit, 0, keepdims=False)
        sending = lax.dynamic_index_in_dim(split_sum, 1 - which_bit, 0, keepdims=False)
        partial_sum = keeping + partner(sending, "space", bit_number)
    meson_local = partial_sum[0]
    first_block = meson_local[:, 0, :]
    all_first = lax.all_gather(first_block, "cuts", axis=0, tiled=True)
    partner_slice = partners[slice_index]
    partner_block = lax.dynamic_slice_in_dim(all_first, partner_slice * row_count, row_count, 0)
    product = jnp.einsum(
        "mak,kn->man",
        meson_local,
        lax.all_gather(partner_block, "space", axis=0, tiled=True),
        precision=lax.Precision.HIGHEST,
    )
    product = product * (1.0 / math.sqrt(MODES))
    return (meson_local[None], product[None])


def solution(mesh):
    in_specs = (P(("grp", "cuts"), None, "space"), P(("grp", "cuts"), None, "space"), P(), P())
    out_specs = (P(("grp", "cuts"), "space", None, None), P(("grp", "cuts"), "space", None, None))
    return jax.shard_map(
        on_device, mesh=mesh, in_specs=in_specs, out_specs=out_specs, check_vma=False
    )
```

profile of v0, /device:TPU:13, one launch (start us, length us, event | category | flops | bytes accessed | tf_op | source)
XLA Modules:
  0.0 278.8 jit_solution(10452409322120406318)
XLA Ops:
  7.2 0.0 copy-start.2
  7.2 0.0 all-gather.5.cloned.1.call-start
  7.2 0.7 collective-permute-start.1
  8.0 1.3 constant_dynamic-slice_fusion.1
  9.2 0.2 collective-permute-start
  9.5 1.0 slice_reduce_fusion.2
  10.5 0.2 fusion.13
  10.7 0.5 collective-permute-done
  11.2 0.1 maximum_bitcast_fusion.2
  11.4 0.0 collective-permute-done.1
  11.4 0.0 copy-done.2
  11.4 16.3 %fusion.2 = f32[512,4,1024]{2,0,1:T(8,128)S(1)} fusion(f32[1024,256]{1,0:T(8,128)} %collective-permute-done.1, f32[1024,256]{1,0:T(8,128)S(1)} %bitcast.35, f32[4,512]{1,0:T(4,128)S(1)} %pad_maximum_fusion, f32[512,512]{1,0:T(8,128)S(1)} %maximum_bitcast_fusion.2), kind=kOutput, calls=%fused_computation.5 | convolution fusion | flops 12886474752 | bytes 11542528 | tf_op jit(solution)/shard_map/max,nx->man/dot_general | solution.py:55
  27.7 0.0 copy-start.1
  27.7 2.6 dynamic-slice_bitcast_fusion
  30.3 1.9 copy-done.1
  32.2 1.2 collective-permute-start.2
  33.4 91.1 %collective-permute-done.2 = f32[1,256,4,1024]{3,1,2,0:T(8,128)} collective-permute-done((f32[1,256,4,1024]{3,1,2,0:T(8,128)}, f32[1,256,4,1024]{3,1,2,0:T(8,128)}, u32[]{:S(2)}, u32[]{:S(2)}) %collective-permute-start.2) | collective-permute-done | bytes 4194336 | tf_op jit(solution)/shard_map/ppermute | solution.py:14
  124.5 4.4 %bitcast_add_fusion = f32[1,256,4,1024]{3,1,2,0:T(8,128)S(1)} fusion(f32[1,256,4,1024]{3,1,2,0:T(8,128)} %collective-permute-done.2, f32[2,1,256,4,1024]{4,2,0,3,1:T(8,128)} %bitcast.30, s32[]{:T(128)S(6)} %select_n.124), kind=kLoop, calls=%fused_computation.2 | loop fusion | flops 1048576 | bytes 12582916 | tf_op jit(solution)/shard_map/add | solution.py:63
  128.9 0.0 copy-start
  128.9 2.0 copy-done
  130.9 1.0 slice.19
  132.0 0.0 all-gather.5.cloned.1.call-update
  132.0 0.0 all-gather.7.cloned.1.call-start
  132.1 0.0 copy-done.3
  132.1 0.7 dynamic_slice.24
  133.4 78.5 %all-gather.5.cloned.1.call-done = f32[1024,1,1024]{2,0,1:T(8,128)} async-done(((f32[256,1,1024]{2,0,1:T(8,128)}), f32[1024,1,1024]{2,0,1:T(8,128)}) %all-gather.5.cloned.1.call-update) | async-done | bytes 4194320 | tf_op jit(solution)/shard_map/all_gather | solution.py:66
  211.9 2.3 constant_dynamic-slice_fusion
  214.2 0.0 all-gather.7.cloned.1.call-update
  214.2 6.9 %copy.6 = f32[1,256,4,1024]{3,2,1,0:T(4,128)} copy(f32[1,256,4,1024]{3,1,2,0:T(8,128)} %copy-done) | data formatting | bytes 8388608
  221.1 29.1 %all-gather.7.cloned.1.call-done = f32[1024,1,1024]{2,0,1:T(8,128)} async-done(((f32[256,1,1024]{2,0,1:T(8,128)}), f32[1024,1,1024]{2,0,1:T(8,128)}) %all-gather.7.cloned.1.call-update) | async-done | bytes 4194320 | tf_op jit(solution)/shard_map/all_gather | solution.py:72
  250.2 17.1 %multiply_bitcast_fusion = f32[1,256,4,1024]{3,1,2,0:T(8,128)S(1)} fusion(f32[1024,1,1024]{2,0,1:T(8,128)} %all-gather.7.cloned.1.call-done, f32[1,256,4,1024]{3,1,2,0:T(8,128)} %copy-done), kind=kOutput, calls=%fused_computation.3 | convolution fusion | flops 12885950464 | bytes 12582912 | tf_op jit(solution)/shard_map/mak,kn->man/dot_general | solution.py:69
  267.3 4.7 %copy.7 = f32[1,256,4,1024]{3,2,1,0:T(4,128)} copy(f32[1,256,4,1024]{3,1,2,0:T(8,128)S(1)} %multiply_bitcast_fusion) | data formatting | bytes 8388608
  (5 shorter events, 0.1 us)
Async XLA Ops:
  7.2 4.2 %copy-start.2 = (f32[1,1024,256]{2,1,0:T(8,128)S(1)}, f32[1,1024,256]{2,1,0:T(8,128)}, u32[]{:S(2)}) copy-start(f32[1,1024,256]{2,1,0:T(8,128)} %param.5) | copy-start | bytes 3145732
  7.2 204.7 %all-gather.5.cloned.1.call-start = ((), (), s32[]{:S(2)}) async-start(), calls=%async_computation | async-start | bytes 5242880 | tf_op jit(solution)/shard_map/all_gather | solution.py:66
  7.2 4.1 %collective-permute-start.1 = (f32[1024,256]{1,0:T(8,128)}, f32[1024,256]{1,0:T(8,128)}, u32[]{:S(2)}, u32[]{:S(2)}) collective-permute-start(f32[1024,256]{1,0:T(8,128)} %bitcast.34), channel_id=1, source_target_pairs={{0,1},{1,0},{2,3},{3,2},{4,5},{5,4},{6,7},{7,6},{8,9},{9,8},{10,11... | collective-permute-start | bytes 3145736 | tf_op jit(solution)/shard_map/ppermute | solution.py:14
  9.2 2.0 collective-permute-start
  27.7 4.5 %copy-start.1 = (f32[512,4,1024]{2,0,1:T(8,128)}, f32[512,4,1024]{2,0,1:T(8,128)S(1)}, u32[]{:S(2)}) copy-start(f32[512,4,1024]{2,0,1:T(8,128)S(1)} %fusion.2) | copy-start | bytes 25165828
  32.2 92.3 %collective-permute-start.2 = (f32[1,256,4,1024]{3,1,2,0:T(8,128)}, f32[1,256,4,1024]{3,1,2,0:T(8,128)}, u32[]{:S(2)}, u32[]{:S(2)}) collective-permute-start(f32[1,256,4,1024]{3,1,2,0:T(8,128)} %dynamic-slice_bitcast_fusion), channel_id=1, source_target_pairs={{0,2},{1,3},{2,0},{3,1},{4,6},{5,7},{6,4},{7,5},{8,10},{9,11},{10,... | collective-permute-start | bytes 12582920 | tf_op jit(solution)/shard_map/ppermute | solution.py:14
  33.4 98.7 %copy-start.3 = (s32[4]{0:T(128)S(1)}, s32[4]{0:T(128)}, u32[]{:S(2)}) copy-start(s32[4]{0:T(128)} %param.7) | copy-start | bytes 52
  128.9 2.0 copy-start
  132.0 118.2 %all-gather.7.cloned.1.call-start = ((), (), s32[]{:S(2)}) async-start(), calls=%async_computation.1 | async-start | bytes 5242880 | tf_op jit(solution)/shard_map/all_gather | solution.py:72
Sparse Core Ops, SparseCore 0:
  132.1 79.7 all-gather.4
  214.3 35.8 all-gather.6
where the time goes:
time: 280 us; the launch traced here: 279 us
  waiting for transfers between devices  199 us (71%)
  matrix products  33.4 us (12%)
  local copies, waits for them, and re-layouts  24.4 us (9%)
  between operations  14.8 us (5%)
  other arithmetic  4.75 us (2%)
    ppermute x3, waiting for transfers between devices, partner(): return lax.ppermute(value, axis, pairs)  91.6 us
    all_gather x1, waiting for transfers between devices, on_device(): all_first = lax.all_gather(first_block, 'cuts', axis=0, tiled=True)  78.5 us
    all_gather x1, waiting for transfers between devices, on_device(): lax.all_gather(partner_block, 'space', axis=0, tiled=True)  29.1 us
    dot_general x1, matrix products, on_device(): jnp.einsum('mak,kn->man', meson_local, lax.all_gather(partner_block, 'spa...  17.1 us
    dot_general x1, matrix products, on_device(): jnp.einsum('max,nx->man', weighted, right_pair, precision=lax.Precision.H...  16.3 us
    unnamed x10, local copies, waits for them, and re-layouts  15.5 us
  transfers between devices with their start and end apart: 5, of which 4 were waited for; matrix products, arithmetic and copies ran while one was open for 4% of the time, Pallas kernels for 0%

commit v1 on v0

v1 whole, which is shorter than its diff:
```python
import functools
import math

import jax
import jax.numpy as jnp
from jax import lax
from jax.experimental import pallas as pl
from jax.experimental.pallas import tpu as pltpu
from jax.sharding import PartitionSpec as P

MODES = 1024
CHUNKS = 4


def phase_table(momenta, site_total):
    global_site = jnp.arange(site_total, dtype=jnp.int32)
    coord_x = global_site % 8
    coord_y = global_site // 8 % 8
    coord_z = global_site // 64
    depth = site_total // 64
    numerator = (
        (momenta[:, 0:1] * coord_x[None] + momenta[:, 1:2] * coord_y[None]) * depth
        + momenta[:, 2:3] * coord_z[None] * 8
    ) % (8 * depth)
    return jnp.cos(2.0 * math.pi * numerator.astype(jnp.float32) / (8 * depth))


def split(value):
    high = value.astype(jnp.bfloat16)
    return high, (value - high.astype(jnp.float32)).astype(jnp.bfloat16)


def dot3(a_high, a_low, b_high, b_low, b_axis):
    dims = (((1,), (b_axis,)), ((), ()))
    dot = functools.partial(
        lax.dot_general, dimension_numbers=dims, preferred_element_type=jnp.float32
    )
    return dot(a_low, b_high) + dot(a_high, b_low) + dot(a_high, b_high)


def kernel(
    slices, space_size, scale,
    partners_ref, phase_ref, left_ref, right_ref,
    meson_ref, product_ref,
    left_far, left_peer, right_far, right_peer,
    w_high, w_low, r_high, r_low, m_high, m_low,
    route, field_far, field_peer, f_high, f_low,
    lf_sem, lp_sem, rf_sem, rp_sem, z_sem, ff_sem, fp_sem,
):
    mode_total, site_local = left_ref.shape
    verts = phase_ref.shape[0]
    rows = mode_total // space_size
    chips = space_size // 2
    width = mode_total // CHUNKS
    far = range(1, chips)

    me = lax.axis_index("space")
    zed = lax.axis_index("cuts")
    chip, core = me // 2, me % 2
    peer = chip * 2 + 1 - core

    def far_device(d):
        return lax.rem(chip + d, chips) * 2 + core

    def source(d, k):
        from_chip = lax.rem(chip + chips - d, chips)
        return from_chip * 2 + (core if k == 0 else 1 - core)

    def remote(src, dst, sems, where, axis, target):
        return pltpu.make_async_remote_copy(
            src_ref=src,
            dst_ref=dst,
            send_sem=sems.at[(0,) + where],
            recv_sem=sems.at[(1,) + where],
            device_id={axis: target},
            device_id_type=pl.DeviceIdType.MESH,
        )

    barrier = pltpu.get_barrier_semaphore()

    def greet(axis, target):
        pl.semaphore_signal(
            barrier, inc=1, device_id={axis: target}, device_id_type=pl.DeviceIdType.MESH
        )

    greet("space", peer)
    for d in far:
        greet("space", far_device(d))

    @pl.when(zed > 0)
    def _():
        greet("cuts", zed - 1)

    @pl.when(zed < slices - 1)
    def _():
        greet("cuts", zed + 1)

    ends = jnp.where(zed > 0, 1, 0) + jnp.where(zed < slices - 1, 1, 0)
    pl.semaphore_wait(barrier, chips + ends)

    def rows_of(ref, index, count):
        return ref.at[pl.ds(pl.multiple_of(index * count, count), count), :]

    def chunk_of(ref, j):
        return ref.at[pl.ds(j * width, width), :]

    left_far_copy = {
        d: remote(
            rows_of(left_ref, lax.rem(chip + d, chips), 2 * rows),
            left_far.at[d - 1], lf_sem, (d - 1,), "space", far_device(d),
        )
        for d in far
    }
    right_far_copy = {
        (d, j): remote(
            chunk_of(right_ref, j), chunk_of(right_far.at[d - 1], j),
            rf_sem, (d - 1, j), "space", far_device(d),
        )
        for d in far for j in range(CHUNKS)
    }
    left_peer_copy = {
        d: remote(
            rows_of(left_ref, peer, rows) if d == 0 else rows_of(left_far.at[d - 1], 1 - core, rows),
            left_peer.at[d], lp_sem, (d,), "space", peer,
        )
        for d in range(chips)
    }
    right_peer_copy = {
        (d, j): remote(
            chunk_of(right_ref if d == 0 else right_far.at[d - 1], j),
            chunk_of(right_peer.at[d], j), rp_sem, (d, j), "space", peer,
        )
        for d in range(chips) for j in range(CHUNKS)
    }

    def z_copy(j, r):
        up = zed % 2 == r % 2
        other = jnp.where(up, zed + 1, zed - 1)
        has = (other >= 0) & (other < slices)
        return has, remote(route.at[j, r, 0], route.at[j, r, 1], z_sem, (j, r), "cuts", other)

    field_far_copy = {
        (d, j): remote(
            route.at[j, slices, 0], field_far.at[j, d - 1], ff_sem, (d - 1, j), "space", far_device(d)
        )
        for d in far for j in range(CHUNKS)
    }
    field_peer_copy = {
        (d, j): remote(
            route.at[j, slices, 0] if d == 0 else field_far.at[j, d - 1],
            field_peer.at[j, d], fp_sem, (d, j), "space", peer,
        )
        for d in range(chips) for j in range(CHUNKS)
    }

    for d in far:
        left_far_copy[d].start()
    left_peer_copy[0].start()
    for j in range(CHUNKS):
        for d in far:
            right_far_copy[d, j].start()
        right_peer_copy[0, j].start()

    keys = []
    for u in range(slices):
        key = jnp.int32(0)
        for t in range(slices):
            key = key + jnp.where(partners_ref[t] == u, t, 0)
        keys.append(key)
    takes = []
    for r in range(slices):
        take = jnp.int32(0)
        for i in range(r % 2, slices - 1, 2):
            low, high = jnp.minimum(keys[i], keys[i + 1]), jnp.maximum(keys[i], keys[i + 1])
            swap = jnp.where(keys[i] > keys[i + 1], 1, 0)
            mine = jnp.where((zed == i) | (zed == i + 1), 1, 0)
            take = take + swap * mine
            keys[i], keys[i + 1] = low, high
        takes.append(take)

    def weigh(d, k, block):
        at = (2 * d + k) * site_local
        first = pl.multiple_of(source(d, k) * site_local, site_local)
        for a in range(verts):
            high, low = split(block * phase_ref[pl.ds(a, 1), pl.ds(first, site_local)])
            w_high[a, :, pl.ds(at, site_local)] = high
            w_low[a, :, pl.ds(at, site_local)] = low

    def own_rows(ref, index):
        return ref[pl.ds(pl.multiple_of(index * rows, rows), rows), :]

    weigh(0, 0, own_rows(left_ref, me))
    left_peer_copy[0].wait_recv()
    weigh(0, 1, left_peer[0])
    for d in far:
        left_far_copy[d].wait_recv()
        left_peer_copy[d].start()
        weigh(d, 0, own_rows(left_far.at[d - 1], core))
    for d in far:
        left_peer_copy[d].wait_recv()
        weigh(d, 1, left_peer[d])

    def split_right(d, k, block):
        at = (2 * d + k) * site_local
        high, low = split(block)
        r_high[:, pl.ds(at, site_local)] = high
        r_low[:, pl.ds(at, site_local)] = low

    def meson_block(a, j):
        block = dot3(w_high[a], w_low[a], r_high[...], r_low[...], 1)
        columns = pl.ds(j * width, width)
        meson_ref[a, :, columns] = block
        high, low = split(block)
        m_high[a, :, columns] = high
        m_low[a, :, columns] = low
        return block

    def z_start(j, r):
        has, copy = z_copy(j, r)

        @pl.when(has)
        def _():
            copy.start()

    def fields(j):
        split_right(0, 0, right_ref[pl.ds(j * width, width), :])
        right_peer_copy[0, j].wait_recv()
        split_right(0, 1, right_peer[0, pl.ds(j * width, width), :])
        for d in far:
            right_far_copy[d, j].wait_recv()
            right_peer_copy[d, j].start()
            split_right(d, 0, right_far[d - 1, pl.ds(j * width, width), :])
        for d in far:
            right_peer_copy[d, j].wait_recv()
            split_right(d, 1, right_peer[d, pl.ds(j * width, width), :])
        route[j, 0, 0] = meson_block(0, j)
        z_start(j, 0)

        def other_vertex(a, carry):
            meson_block(a, j)
            return carry

        lax.fori_loop(1, verts, other_vertex, 0)

    def z_round(j, r):
        has, copy = z_copy(j, r)

        @pl.when(has)
        def _():
            copy.wait_recv()
            taken = jnp.full((rows, width), takes[r], jnp.int32) > 0
            route[j, r + 1, 0] = jnp.where(taken, route[j, r, 1], route[j, r, 0])

        @pl.when(jnp.logical_not(has))
        def _():
            route[j, r + 1, 0] = route[j, r, 0]

        if r + 1 < slices:
            z_start(j, r + 1)
        else:
            for d in far:
                field_far_copy[d, j].start()
            field_peer_copy[0, j].start()

    def pass_on(j):
        for d in far:
            field_far_copy[d, j].wait_recv()
            field_peer_copy[d, j].start()

    def products(j):
        def place(d, k, block):
            first = pl.multiple_of(source(d, k) * rows, rows)
            high, low = split(block)
            f_high[pl.ds(first, rows), :] = high
            f_low[pl.ds(first, rows), :] = low

        place(0, 0, route[j, slices, 0])
        for d in far:
            place(d, 0, field_far[j, d - 1])
        for d in range(chips):
            field_peer_copy[d, j].wait_recv()
            place(d, 1, field_peer[j, d])

        def vertex(a, carry):
            block = dot3(m_high[a], m_low[a], f_high[...], f_low[...], 0)
            product_ref[a, :, pl.ds(j * width, width)] = block * scale
            return carry

        lax.fori_loop(0, verts, vertex, 0)

    for step in range(CHUNKS + slices + 2):
        if step < CHUNKS:
            fields(step)
        for r in reversed(range(slices)):
            if 0 <= step - 1 - r < CHUNKS:
                z_round(step - 1 - r, r)
        if 0 <= step - 1 - slices < CHUNKS:
            pass_on(step - 1 - slices)
        if 0 <= step - 2 - slices < CHUNKS:
            products(step - 2 - slices)

    for copies in (
        left_far_copy, right_far_copy, left_peer_copy, right_peer_copy,
        field_far_copy, field_peer_copy,
    ):
        for copy in copies.values():
            copy.wait_send()
    for j in range(CHUNKS):
        for r in range(slices):
            has, copy = z_copy(j, r)

            @pl.when(has)
            def _(copy=copy):
                copy.wait_send()


def on_device(left_modes, right_modes, momenta, partners):
    left_local, right_local = left_modes[0], right_modes[0]
    mode_total, site_local = left_local.shape
    space_size = lax.axis_size("space")
    slices = lax.axis_size("cuts")
    verts = momenta.shape[0]
    rows = mode_total // space_size
    chips = space_size // 2
    others = max(chips - 1, 1)
    width = mode_total // CHUNKS
    depth = site_local * space_size
    phases = phase_table(momenta, depth)
    f32, bf16 = jnp.float32, jnp.bfloat16
    vmem = pl.BlockSpec(memory_space=pltpu.VMEM)
    out = jax.ShapeDtypeStruct((verts, rows, mode_total), f32)

    def dma(*shape):
        return pltpu.SemaphoreType.DMA((2,) + shape)

    meson, product = pl.pallas_call(
        functools.partial(kernel, slices, space_size, 1.0 / math.sqrt(mode_total)),
        out_shape=(out, out),
        in_specs=[pl.BlockSpec(memory_space=pltpu.SMEM), vmem, vmem, vmem],
        out_specs=(vmem, vmem),
        scratch_shapes=[
            pltpu.VMEM((others, 2 * rows, site_local), f32),
            pltpu.VMEM((chips, rows, site_local), f32),
            pltpu.VMEM((others, mode_total, site_local), f32),
            pltpu.VMEM((chips, mode_total, site_local), f32),
            pltpu.VMEM((verts, rows, depth), bf16),
            pltpu.VMEM((verts, rows, depth), bf16),
            pltpu.VMEM((width, depth), bf16),
            pltpu.VMEM((width, depth), bf16),
            pltpu.VMEM((verts, rows, mode_total), bf16),
            pltpu.VMEM((verts, rows, mode_total), bf16),
            pltpu.VMEM((CHUNKS, slices + 1, 2, rows, width), f32),
            pltpu.VMEM((CHUNKS, others, rows, width), f32),
            pltpu.VMEM((CHUNKS, chips, rows, width), f32),
            pltpu.VMEM((mode_total, width), bf16),
            pltpu.VMEM((mode_total, width), bf16),
            dma(others), dma(chips), dma(others, CHUNKS), dma(chips, CHUNKS),
            dma(CHUNKS, slices), dma(others, CHUNKS), dma(chips, CHUNKS),
        ],
        compiler_params=pltpu.CompilerParams(
            collective_id=0, has_side_effects=True, vmem_limit_bytes=58 * 2**20
        ),
    )(partners, phases, left_local, right_local)
    return (meson.transpose(1, 0, 2)[None], product.transpose(1, 0, 2)[None])


def solution(mesh):
    in_specs = (P(("grp", "cuts"), None, "space"), P(("grp", "cuts"), None, "space"), P(), P())
    out_specs = (P(("grp", "cuts"), "space", None, None), P(("grp", "cuts"), "space", None, None))
    return jax.shard_map(
        on_device, mesh=mesh, in_specs=in_specs, out_specs=out_specs, check_vma=False
    )
```

time: 280 us -> 117 us (0.42)
  waiting for transfers between devices: 199 us -> 0 us
  Pallas kernels: 0 us -> 101 us
  matrix products: 33.4 us -> 0 us
  between operations: 14.8 us -> 0.66 us
  local copies, waits for them, and re-layouts: 24.4 us -> 12.8 us
  other arithmetic: 4.75 us -> 0.83 us
    all_gather x2 -> x0, waiting for transfers between devices: 108 us -> none  [the longest x1 78.5 us: on_device(): all_first = lax.all_gather(first_block, 'cuts', axis=0, tiled=True)]
    pallas_call x0 -> x1, Pallas kernels: none -> 101 us  [on_device(): pl.pallas_call(functools.partial(kernel, slices, space_size, 1.0 / math.s...]
    ppermute x3 -> x0, waiting for transfers between devices: 91.6 us -> none  [partner(): return lax.ppermute(value, axis, pairs)]
    dot_general x2 -> x0, matrix products: 33.4 us -> none  [the longest x1 17.1 us: on_device(): jnp.einsum('mak,kn->man', meson_local, lax.all_gather(partner_block, 'spa...]
    add x1 -> x0, other arithmetic: 4.4 us -> none  [on_device(): partial_sum = keeping + partner(sending, 'space', bit_number)]
    dynamic_slice x3 -> x0, local copies, waits for them, and re-layouts: 4.22 us -> none  [the longest x1 2.3 us: on_device(): lax.dynamic_slice_in_dim(all_first, partner_slice * row_count, row_count, 0)]
    unnamed x10 -> x4, local copies, waits for them, and re-layouts: 15.5 us -> 11.8 us
  transfers between devices with their start and end apart: 5 -> 0, of which waited for: 4 -> 0; matrix products, arithmetic and copies ran while one was open for 4% -> 0% of each run, Pallas kernels for 0% -> 0%
where the time goes in v1:
time: 117 us; the launch traced here: 115 us
  Pallas kernels  101 us (86%)
  local copies, waits for them, and re-layouts  12.8 us (11%)
    pallas_call x1, Pallas kernels, on_device(): pl.pallas_call(functools.partial(kernel, slices, space_size, 1.0 / math.s...  101 us
    unnamed x4, local copies, waits for them, and re-layouts  11.8 us

profile of v1, /device:TPU:13, one launch (start us, length us, event | category | flops | bytes accessed | tf_op | source)
XLA Modules:
  0.0 114.8 jit_solution(6048927959071424347)
XLA Ops:
  0.6 1.0 slice_reduce_fusion.2
  1.7 0.8 fusion.3.phase_ref
  2.5 100.5 %shard_map.59 = (f32[4,256,1024]{2,1,0:T(8,128)}, f32[4,256,1024]{2,1,0:T(8,128)}) custom-call(s32[4]{0:T(128)} %partners_ref.1, f32[4,1024]{1,0:T(4,128)} %fusion.3.phase_ref, f32[1024,256]{1,0:T(8,128)} %bitcast.10, f32[1024,256]{1,0:T(8,128)} %bitcast.11), custom_call_target="tpu_custom_call" | custom-call | tf_op jit(solution)/shard_map/pallas_call | solution.py:336
  103.0 0.0 copy-start
  103.0 7.0 %copy.6 = f32[1,256,4,1024]{3,2,1,0:T(4,128)} copy(f32[1,256,4,1024]{3,1,2,0:T(8,128)} %bitcast.9) | data formatting | bytes 8388608
  110.1 0.0 copy-done
  110.1 4.7 %copy.7 = f32[1,256,4,1024]{3,2,1,0:T(4,128)} copy(f32[1,256,4,1024]{3,1,2,0:T(8,128)S(1)} %bitcast.8) | data formatting | bytes 8388608
  (2 shorter events, 0.0 us)
Async XLA Ops:
  103.0 7.1 %copy-start = (f32[4,256,1024]{2,1,0:T(8,128)S(1)}, f32[4,256,1024]{2,1,0:T(8,128)}, u32[]{:S(2)}) copy-start(f32[4,256,1024]{2,1,0:T(8,128)} %get-tuple-element.5) | copy-start | bytes 12582916

commit v2 on v1

--- a/solution.py
+++ b/solution.py
@@ -9,7 +9,8 @@
 from jax.sharding import PartitionSpec as P
 
 MODES = 1024
-CHUNKS = 4
+CHUNKS = 8
+PAIR = 2
 
 
 def phase_table(momenta, site_total):
@@ -42,10 +43,11 @@
     slices, space_size, scale,
     partners_ref, phase_ref, left_ref, right_ref,
     meson_ref, product_ref,
+    m_held, p_held,
     left_far, left_peer, right_far, right_peer,
     w_high, w_low, r_high, r_low, m_high, m_low,
     route, field_far, field_peer, f_high, f_low,
-    lf_sem, lp_sem, rf_sem, rp_sem, z_sem, ff_sem, fp_sem,
+    lf_sem, lp_sem, rf_sem, rp_sem, z_sem, ff_sem, fp_sem, m_sem, p_sem,
 ):
     mode_total, site_local = left_ref.shape
     verts = phase_ref.shape[0]
@@ -157,9 +159,15 @@
         left_far_copy[d].start()
     left_peer_copy[0].start()
     for j in range(CHUNKS):
-        for d in far:
-            right_far_copy[d, j].start()
         right_peer_copy[0, j].start()
+
+    def send_right(*chunks):
+        for j in chunks:
+            for d in far:
+                if j < CHUNKS:
+                    right_far_copy[d, j].start()
+
+    send_right(0)
 
     keys = []
     for u in range(slices):
@@ -195,21 +203,24 @@
     for d in far:
         left_far_copy[d].wait_recv()
         left_peer_copy[d].start()
+        if d == chips - 1:
+            send_right(1, 2)
         weigh(d, 0, own_rows(left_far.at[d - 1], core))
     for d in far:
         left_peer_copy[d].wait_recv()
         weigh(d, 1, left_peer[d])
 
-    def split_right(d, k, block):
+    def split_right(d, k, j, block):
         at = (2 * d + k) * site_local
         high, low = split(block)
-        r_high[:, pl.ds(at, site_local)] = high
-        r_low[:, pl.ds(at, site_local)] = low
-
-    def meson_block(a, j):
-        block = dot3(w_high[a], w_low[a], r_high[...], r_low[...], 1)
-        columns = pl.ds(j * width, width)
-        meson_ref[a, :, columns] = block
+        r_high[pl.ds(j % PAIR * width, width), pl.ds(at, site_local)] = high
+        r_low[pl.ds(j % PAIR * width, width), pl.ds(at, site_local)] = low
+
+    def meson_block(a, j, count):
+        some = pl.ds(j % PAIR * width, count * width)
+        block = dot3(w_high[a], w_low[a], r_high[some, :], r_low[some, :], 1)
+        columns = pl.ds(j * width, count * width)
+        m_held[a, :, columns] = block
         high, low = split(block)
         m_high[a, :, columns] = high
         m_low[a, :, columns] = low
@@ -223,24 +234,35 @@
             copy.start()
 
     def fields(j):
-        split_right(0, 0, right_ref[pl.ds(j * width, width), :])
+        split_right(0, 0, j, right_ref[pl.ds(j * width, width), :])
         right_peer_copy[0, j].wait_recv()
-        split_right(0, 1, right_peer[0, pl.ds(j * width, width), :])
+        split_right(0, 1, j, right_peer[0, pl.ds(j * width, width), :])
         for d in far:
             right_far_copy[d, j].wait_recv()
             right_peer_copy[d, j].start()
-            split_right(d, 0, right_far[d - 1, pl.ds(j * width, width), :])
+            if d == chips - 1 and j > 0:
+                send_right(j + 2)
+            split_right(d, 0, j, right_far[d - 1, pl.ds(j * width, width), :])
         for d in far:
             right_peer_copy[d, j].wait_recv()
-            split_right(d, 1, right_peer[d, pl.ds(j * width, width), :])
-        route[j, 0, 0] = meson_block(0, j)
+            split_right(d, 1, j, right_peer[d, pl.ds(j * width, width), :])
+        route[j, 0, 0] = meson_block(0, j, 1)
         z_start(j, 0)
 
+    def out_copy(held, ref, sems, a, g):
+        columns = pl.ds(g * PAIR * width, PAIR * width)
+        return pltpu.make_async_copy(
+            held.at[a, :, columns], ref.at[:, a, columns], sems.at[a, g]
+        )
+
+    def other_fields(g):
         def other_vertex(a, carry):
-            meson_block(a, j)
+            meson_block(a, g * PAIR, PAIR)
             return carry
 
         lax.fori_loop(1, verts, other_vertex, 0)
+        for a in range(verts):
+            out_copy(m_held, meson_ref, m_sem, a, g).start()
 
     def z_round(j, r):
         has, copy = z_copy(j, r)
@@ -267,12 +289,12 @@
             field_far_copy[d, j].wait_recv()
             field_peer_copy[d, j].start()
 
-    def products(j):
+    def gathered(j):
         def place(d, k, block):
             first = pl.multiple_of(source(d, k) * rows, rows)
             high, low = split(block)
-            f_high[pl.ds(first, rows), :] = high
-            f_low[pl.ds(first, rows), :] = low
+            f_high[pl.ds(first, rows), pl.ds(j % PAIR * width, width)] = high
+            f_low[pl.ds(first, rows), pl.ds(j % PAIR * width, width)] = low
 
         place(0, 0, route[j, slices, 0])
         for d in far:
@@ -281,12 +303,15 @@
             field_peer_copy[d, j].wait_recv()
             place(d, 1, field_peer[j, d])
 
+    def products(g):
         def vertex(a, carry):
             block = dot3(m_high[a], m_low[a], f_high[...], f_low[...], 0)
-            product_ref[a, :, pl.ds(j * width, width)] = block * scale
+            p_held[a, :, pl.ds(g * PAIR * width, PAIR * width)] = block * scale
             return carry
 
         lax.fori_loop(0, verts, vertex, 0)
+        for a in range(verts):
+            out_copy(p_held, product_ref, p_sem, a, g).start()
 
     for step in range(CHUNKS + slices + 2):
         if step < CHUNKS:
@@ -296,9 +321,18 @@
                 z_round(step - 1 - r, r)
         if 0 <= step - 1 - slices < CHUNKS:
             pass_on(step - 1 - slices)
-        if 0 <= step - 2 - slices < CHUNKS:
-            products(step - 2 - slices)
-
+        if step < CHUNKS and step % PAIR == PAIR - 1:
+            other_fields(step // PAIR)
+        j = step - 2 - slices
+        if 0 <= j < CHUNKS:
+            gathered(j)
+            if j % PAIR == PAIR - 1:
+                products(j // PAIR)
+
+    for g in range(CHUNKS // PAIR):
+        for a in range(verts):
+            out_copy(m_held, meson_ref, m_sem, a, g).wait()
+            out_copy(p_held, product_ref, p_sem, a, g).wait()
     for copies in (
         left_far_copy, right_far_copy, left_peer_copy, right_peer_copy,
         field_far_copy, field_peer_copy,
@@ -328,7 +362,8 @@
     phases = phase_table(momenta, depth)
     f32, bf16 = jnp.float32, jnp.bfloat16
     vmem = pl.BlockSpec(memory_space=pltpu.VMEM)
-    out = jax.ShapeDtypeStruct((verts, rows, mode_total), f32)
+    out = jax.ShapeDtypeStruct((rows, verts, mode_total), f32)
+    hbm = pl.BlockSpec(memory_space=pl.ANY)
 
     def dma(*shape):
         return pltpu.SemaphoreType.DMA((2,) + shape)
@@ -337,31 +372,35 @@
         functools.partial(kernel, slices, space_size, 1.0 / math.sqrt(mode_total)),
         out_shape=(out, out),
         in_specs=[pl.BlockSpec(memory_space=pltpu.SMEM), vmem, vmem, vmem],
-        out_specs=(vmem, vmem),
+        out_specs=(hbm, hbm),
         scratch_shapes=[
+            pltpu.VMEM((verts, rows, mode_total), f32),
+            pltpu.VMEM((verts, rows, mode_total), f32),
             pltpu.VMEM((others, 2 * rows, site_local), f32),
             pltpu.VMEM((chips, rows, site_local), f32),
             pltpu.VMEM((others, mode_total, site_local), f32),
             pltpu.VMEM((chips, mode_total, site_local), f32),
             pltpu.VMEM((verts, rows, depth), bf16),
             pltpu.VMEM((verts, rows, depth), bf16),
-            pltpu.VMEM((width, depth), bf16),
-            pltpu.VMEM((width, depth), bf16),
+            pltpu.VMEM((PAIR * width, depth), bf16),
+            pltpu.VMEM((PAIR * width, depth), bf16),
             pltpu.VMEM((verts, rows, mode_total), bf16),
             pltpu.VMEM((verts, rows, mode_total), bf16),
             pltpu.VMEM((CHUNKS, slices + 1, 2, rows, width), f32),
             pltpu.VMEM((CHUNKS, others, rows, width), f32),
             pltpu.VMEM((CHUNKS, chips, rows, width), f32),
-            pltpu.VMEM((mode_total, width), bf16),
-            pltpu.VMEM((mode_total, width), bf16),
+            pltpu.VMEM((mode_total, PAIR * width), bf16),
+            pltpu.VMEM((mode_total, PAIR * width), bf16),
             dma(others), dma(chips), dma(others, CHUNKS), dma(chips, CHUNKS),
             dma(CHUNKS, slices), dma(others, CHUNKS), dma(chips, CHUNKS),
+            pltpu.SemaphoreType.DMA((verts, CHUNKS // PAIR)),
+            pltpu.SemaphoreType.DMA((verts, CHUNKS // PAIR)),
         ],
         compiler_params=pltpu.CompilerParams(
             collective_id=0, has_side_effects=True, vmem_limit_bytes=58 * 2**20
         ),
     )(partners, phases, left_local, right_local)
-    return (meson.transpose(1, 0, 2)[None], product.transpose(1, 0, 2)[None])
+    return (meson[None], product[None])
 
 
 def solution(mesh):

time: 117 us -> 104 us (0.89); the launches traced: 115 us -> 104 us
  Pallas kernels: 101 us -> 93.7 us
  local copies, waits for them, and re-layouts: 12.8 us -> 8.36 us
    pallas_call x1, Pallas kernels: 101 us -> 93.7 us  [on_device(): pl.pallas_call(functools.partial(kernel, slices, space_size, 1.0 / math.s...]
    unnamed x4, local copies, waits for them, and re-layouts: 11.8 us -> 7.36 us
where the time goes in v2:
time: 104 us
  Pallas kernels  93.7 us (90%)
  local copies, waits for them, and re-layouts  8.36 us (8%)
    pallas_call x1, Pallas kernels, on_device(): pl.pallas_call(functools.partial(kernel, slices, space_size, 1.0 / math.s...  93.7 us
    unnamed x4, local copies, waits for them, and re-layouts  7.36 us

profile of v2, /device:TPU:13, one launch (start us, length us, event | category | flops | bytes accessed | tf_op | source)
XLA Modules:
  0.0 103.6 jit_solution(13216533210304874620)
XLA Ops:
  0.6 1.0 slice_reduce_fusion.2
  1.7 0.8 fusion.3.phase_ref
  2.5 93.7 %shard_map.59 = (f32[256,4,1024]{2,1,0:T(4,128)}, f32[256,4,1024]{2,1,0:T(4,128)}) custom-call(s32[4]{0:T(128)} %partners_ref.1, f32[4,1024]{1,0:T(4,128)} %fusion.3.phase_ref, f32[1024,256]{1,0:T(8,128)} %bitcast.6, f32[1024,256]{1,0:T(8,128)} %bitcast.7), custom_call_target="tpu_custom_call" | custom-call | tf_op jit(solution)/shard_map/pallas_call | solution.py:371
  96.2 0.0 copy-start
  96.2 5.3 %copy.8 = f32[1,256,4,1024]{3,2,1,0:T(4,128)} copy(f32[1,256,4,1024]{3,2,1,0:T(4,128)} %bitcast.5) | data formatting | bytes 8388608
  101.6 0.0 copy-done
  101.6 2.0 %copy.9 = f32[1,256,4,1024]{3,2,1,0:T(4,128)} copy(f32[1,256,4,1024]{3,2,1,0:T(4,128)S(1)} %bitcast.4) | data formatting | bytes 8388608
  (2 shorter events, 0.0 us)
Async XLA Ops:
  96.2 5.4 %copy-start = (f32[256,4,1024]{2,1,0:T(4,128)S(1)}, f32[256,4,1024]{2,1,0:T(4,128)}, u32[]{:S(2)}) copy-start(f32[256,4,1024]{2,1,0:T(4,128)} %get-tuple-element.5) | copy-start | bytes 12582916

commit v3 on v2

--- a/solution.py
+++ b/solution.py
@@ -313,17 +313,17 @@
         for a in range(verts):
             out_copy(p_held, product_ref, p_sem, a, g).start()
 
-    for step in range(CHUNKS + slices + 2):
+    for step in range(CHUNKS + 2 * slices + 2):
         if step < CHUNKS:
             fields(step)
         for r in reversed(range(slices)):
-            if 0 <= step - 1 - r < CHUNKS:
-                z_round(step - 1 - r, r)
-        if 0 <= step - 1 - slices < CHUNKS:
-            pass_on(step - 1 - slices)
+            if 0 <= step - 1 - 2 * r < CHUNKS:
+                z_round(step - 1 - 2 * r, r)
+        if 0 <= step - 2 - 2 * (slices - 1) < CHUNKS:
+            pass_on(step - 2 - 2 * (slices - 1))
         if step < CHUNKS and step % PAIR == PAIR - 1:
             other_fields(step // PAIR)
-        j = step - 2 - slices
+        j = step - 3 - 2 * (slices - 1)
         if 0 <= j < CHUNKS:
             gathered(j)
             if j % PAIR == PAIR - 1:

time: 104 us -> 102 us (0.981)
  Pallas kernels: 93.7 us -> 91.4 us
    pallas_call x1, Pallas kernels: 93.7 us -> 91.4 us  [on_device(): pl.pallas_call(functools.partial(kernel, slices, space_size, 1.0 / math.s...]
where the time goes in v3:
time: 102 us; the launch traced here: 101 us
  Pallas kernels  91.4 us (90%)
  local copies, waits for them, and re-layouts  8.36 us (8%)
    pallas_call x1, Pallas kernels, on_device(): pl.pallas_call(functools.partial(kernel, slices, space_size, 1.0 / math.s...  91.4 us
    unnamed x4, local copies, waits for them, and re-layouts  7.36 us

profile of v3, /device:TPU:13, one launch (start us, length us, event | category | flops | bytes accessed | tf_op | source)
XLA Modules:
  0.0 101.2 jit_solution(10847950828776440298)
XLA Ops:
  0.6 1.0 slice_reduce_fusion.2
  1.7 0.8 fusion.3.phase_ref
  2.5 91.4 %shard_map.59 = (f32[256,4,1024]{2,1,0:T(4,128)}, f32[256,4,1024]{2,1,0:T(4,128)}) custom-call(s32[4]{0:T(128)} %partners_ref.1, f32[4,1024]{1,0:T(4,128)} %fusion.3.phase_ref, f32[1024,256]{1,0:T(8,128)} %bitcast.6, f32[1024,256]{1,0:T(8,128)} %bitcast.7), custom_call_target="tpu_custom_call" | custom-call | tf_op jit(solution)/shard_map/pallas_call | solution.py:371
  93.9 0.0 copy-start
  93.9 5.3 %copy.8 = f32[1,256,4,1024]{3,2,1,0:T(4,128)} copy(f32[1,256,4,1024]{3,2,1,0:T(4,128)} %bitcast.5) | data formatting | bytes 8388608
  99.2 0.0 copy-done
  99.2 2.0 %copy.9 = f32[1,256,4,1024]{3,2,1,0:T(4,128)} copy(f32[1,256,4,1024]{3,2,1,0:T(4,128)S(1)} %bitcast.4) | data formatting | bytes 8388608
  (2 shorter events, 0.0 us)
Async XLA Ops:
  93.9 5.4 %copy-start = (f32[256,4,1024]{2,1,0:T(4,128)S(1)}, f32[256,4,1024]{2,1,0:T(4,128)}, u32[]{:S(2)}) copy-start(f32[256,4,1024]{2,1,0:T(4,128)} %get-tuple-element.5) | copy-start | bytes 12582916
